TPU v7x, 32 devices: a whole 2x2x4 slice. The times are simulated.
32 devices in a mesh: groups: 2 (over x), tile: 16 (over z, y, core).
Axes of the slice: x: 2, y: 2, z: 4, core: 2. Of those that a mesh axis runs over, the one named last changes fastest.
Arguments:
- video_latent: bfloat16 [96, 160, 384], P(('groups', 'tile')), parts along dimension 0, may hold values from -6 to 6
- conv_cache: bfloat16 [96, 160, 384], P(('groups', 'tile')), parts along dimension 0, may hold values from -6 to 6
- norm_gain: float32 [384], replicated, may hold values from 0.1 to 1.9
- conv_kernel: bfloat16 [3, 3, 3, 384, 384], replicated, may hold values from -0.0625 to 0.0625
- attend_gain: float32 [384], replicated, may hold values from 0.1 to 1.9
- w_query: bfloat16 [384, 384], replicated, may hold values from -2 to 6
- w_key: bfloat16 [384, 384], replicated, may hold values from -2 to 6
- w_value: bfloat16 [384, 384], replicated, may hold values from -0.3125 to 0.3125
- w_output: bfloat16 [384, 384], replicated, may hold values from -0.3125 to 0.3125
Outputs:
- result: bfloat16 [96, 160, 384], P(('groups', 'tile')), parts along dimension 0
There are 2 independent parts, one for each index of `groups`. A program takes and returns all parts, laid end to end along the dimension named above; an argument that names none is the same for every part. Nothing has to cross between parts.
All inputs are finite; a program needn't handle non-finite values.
Results may differ from a plain program's by a relative error of at most 0.007.
Values may be sent and summed in bfloat16 or wider, within the bound.
A program may use at most 64 MiB of HBM per device.

v0:
```python
import jax
import jax.numpy as jnp
from jax import lax
from jax.sharding import PartitionSpec as P


def from_behind(value, axis, steps):
    count = lax.axis_size(axis)
    pairs = [(source, (source + steps) % count) for source in range(count)]
    return lax.ppermute(value, axis, pairs)


def passed_along(block, axis, distance):
    devices = range(lax.axis_size(axis))
    route = [(i - distance, i) for i in devices if i - distance in devices]
    return lax.ppermute(block, axis, route)


def swapped(value, axis, bit):
    mask = 2**bit
    pairs = [(source, source ^ mask) for source in range(lax.axis_size(axis))]
    return lax.ppermute(value, axis, pairs)


def rms_scale(inputs, scale_gain):
    floats = inputs.astype(jnp.float32)
    return (
        floats * lax.rsqrt(jnp.mean(floats * floats, axis=-1, keepdims=True) + 1e-06) * scale_gain
    )


def body(
    video_latent, conv_cache, norm_gain, conv_kernel, attend_gain, w_query, w_key, w_value, w_output
):
    rows_local, cols_all, channels = video_latent.shape
    tiles = lax.axis_size("tile")
    row_tiles = min(16, tiles // 2)
    row_bits = row_tiles.bit_length() - 1
    frames = tiles // row_tiles
    frame_bits = frames.bit_length() - 1
    position = lax.axis_index("tile")
    time_group = position % frames
    activated = jax.nn.silu(rms_scale(video_latent, norm_gain)).astype(jnp.bfloat16)
    frame_pair = jnp.stack([activated, conv_cache])
    before_one = from_behind(frame_pair, "tile", 1)
    before_two = from_behind(before_one, "tile", 1)
    frame_one = jnp.where(time_group >= 1, before_one[0], before_one[1])
    frame_two = jnp.where(time_group >= 2, before_two[0], before_two[1])
    stacked = jnp.stack([frame_two, frame_one, frame_pair[0]])
    rim_above = passed_along(stacked[:, -1:], "tile", frames)
    rim_below = passed_along(stacked[:, :1], "tile", -frames)
    stacked = jnp.concatenate([rim_above, stacked, rim_below], axis=1)
    padded = jnp.pad(stacked, ((0, 0), (0, 0), (1, 1), (0, 0)))
    summed = jnp.zeros((rows_local * cols_all, channels), jnp.float32)
    for time_tap in range(3):
        for row_tap in range(3):
            for col_tap in range(3):
                window = padded[
                    time_tap, row_tap : row_tap + rows_local, col_tap : col_tap + cols_all
                ]
                summed = summed + jnp.dot(
                    window.reshape(-1, channels),
                    conv_kernel[time_tap, row_tap, col_tap],
                    preferred_element_type=jnp.float32,
                )
    residual = (video_latent.astype(jnp.float32) + summed.reshape(video_latent.shape)).astype(
        jnp.bfloat16
    )
    normed = rms_scale(residual, attend_gain).astype(jnp.bfloat16)
    flat_rows = normed.reshape(-1, channels)
    positions = rows_local * cols_all
    queries = jnp.dot(flat_rows, w_query, preferred_element_type=jnp.float32).astype(jnp.bfloat16)
    score_scale = float(channels) ** (-0.5)
    initial = (
        jnp.full((positions,), -1e30, jnp.float32),
        jnp.zeros((positions,), jnp.float32),
        jnp.zeros((positions, channels), jnp.float32),
    )

    def absorb(running, key_part, value_part):
        highest, weight_sum, numerator = running
        scores = (
            jnp.einsum("qc,kc->qk", queries, key_part, preferred_element_type=jnp.float32)
            * score_scale
        )
        new_highest = jnp.maximum(highest, jnp.max(scores, axis=-1))
        rescale = jnp.exp(highest - new_highest)
        weights = jnp.exp(scores - new_highest[:, None])
        weight_sum = weight_sum * rescale + jnp.sum(weights, axis=-1)
        numerator = numerator * rescale[:, None] + jnp.dot(
            weights.astype(jnp.bfloat16), value_part, preferred_element_type=jnp.float32
        )
        return (new_highest, weight_sum, numerator)

    def project_pair(block_rows):
        key_part = jnp.dot(block_rows, w_key, preferred_element_type=jnp.float32).astype(
            jnp.bfloat16
        )
        value_part = jnp.dot(block_rows, w_value, preferred_element_type=jnp.float32).astype(
            jnp.bfloat16
        )
        return (key_part, value_part)

    keys_local, values_local = project_pair(flat_rows)
    running = absorb(initial, keys_local, values_local)
    held_rows = flat_rows
    for bit_index in range(row_bits):
        partner = swapped(held_rows, "tile", frame_bits + bit_index)
        key_part, value_part = project_pair(partner)
        running = absorb(running, key_part, value_part)
        if bit_index + 1 < row_bits:
            held_rows = jnp.concatenate([held_rows, partner], axis=0)
    highest, weight_sum, numerator = running
    attended = (numerator / weight_sum[:, None]).astype(jnp.bfloat16)
    output_term = jnp.dot(attended, w_output, preferred_element_type=jnp.float32).reshape(
        video_latent.shape
    )
    return (residual.astype(jnp.float32) + output_term).astype(jnp.bfloat16)


def solution(mesh):
    placed = (
        P(("groups", "tile"), None, None),
        P(("groups", "tile"), None, None),
        P(),
        P(),
        P(),
        P(),
        P(),
        P(),
        P(),
    )
    return jax.shard_map(
        body,
        mesh=mesh,
        in_specs=placed,
        out_specs=P(("groups", "tile"), None, None),
        check_vma=False,
    )
```

profile of v0, /device:TPU:0, one launch (start us, length us, event | category | flops | bytes accessed | tf_op | source)
XLA Modules:
  0.0 184.4 jit_solution(8031781905897827496)
XLA Ops:
  0.0 1.2 fusion.52
  1.2 1.3 fusion.209
  2.5 1.1 pad_maximum_fusion.1
  3.6 0.5 collective-permute-start
  4.1 14.1 %collective-permute-done = bf16[2,3,160,384]{3,2,1,0:T(8,128)(2,1)S(1)} collective-permute-done((bf16[2,3,160,384]{3,2,1,0:T(8,128)(2,1)S(1)}, bf16[2,3,160,384]{3,2,1,0:T(8,128)(2,1)S(1)}, u32[]{:S(2)}, u32[]{:S(2)}) %collective-permute-start) | collective-permute-done | bytes 737312 | tf_op jit(solution)/shard_map/ppermute | solution.py:10
  18.3 1.3 fusion.59
  19.6 12.2 %collective-permute-done.1 = bf16[2,3,160,384]{3,2,1,0:T(8,128)(2,1)S(1)} collective-permute-done((bf16[2,3,160,384]{3,2,1,0:T(8,128)(2,1)S(1)}, bf16[2,3,160,384]{3,2,1,0:T(8,128)(2,1)S(1)}, u32[]{:S(2)}, u32[]{:S(2)}) %collective-permute-start.1) | collective-permute-done | bytes 737312 | tf_op jit(solution)/shard_map/ppermute | solution.py:10
  32.0 1.3 collective-permute-start.2
  33.3 1.3 collective-permute-start.3
  34.6 1.3 fusion.76
  36.0 1.3 fusion.94
  37.3 9.1 %collective-permute-done.2 = bf16[3,1,160,384]{3,2,1,0:T(8,128)(2,1)S(1)} collective-permute-done((bf16[3,1,160,384]{3,2,1,0:T(8,128)(2,1)S(1)}, bf16[3,1,160,384]{3,2,1,0:T(8,128)(2,1)S(1)}, u32[]{:S(2)}, u32[]{:S(2)}) %collective-permute-start.2) | collective-permute-done | bytes 368672 | tf_op jit(solution)/shard_map/ppermute | solution.py:16
  46.4 1.7 select_maximum_fusion
  48.2 1.1 fusion.154
  49.3 1.1 slice-done.1
  50.4 0.4 fusion.102
  50.7 0.4 fusion.104
  51.1 0.4 fusion.108
  51.5 0.4 fusion.110
  51.9 0.4 fusion.113
  52.3 0.4 fusion.115
  52.7 0.4 fusion.119
  53.1 0.4 fusion.78
  53.5 0.4 fusion.80
  53.8 0.4 fusion.84
  54.2 0.4 fusion.86
  54.6 0.4 fusion.90
  55.0 0.4 fusion.92
  55.4 0.4 fusion.96
  55.8 0.4 fusion.98
  56.3 0.4 fusion.100
  56.9 0.4 fusion.106
  57.3 0.4 fusion.117
  57.7 0.4 fusion.82
  58.1 0.4 fusion.88
  58.4 0.4 fusion.69
  58.8 0.4 fusion.73
  59.2 0.4 fusion.71
  59.6 1.4 fusion.42
  61.0 0.4 fusion.29
  61.4 0.5 copy-done.1
  62.0 0.2 fusion.61
  62.4 2.5 %collective-permute-start.4 = (bf16[480,384]{1,0:T(8,128)(2,1)S(1)}, bf16[480,384]{1,0:T(8,128)(2,1)S(1)}, u32[]{:S(2)}, u32[]{:S(2)}) collective-permute-start(bf16[480,384]{1,0:T(8,128)(2,1)S(1)} %bitcast.167), channel_id=1, source_target_pairs={{0,2},{1,3},{2,0},{3,1},{4,6},{5,7},{6,4},{7,5},{8,10},{9,11},{10,... | collective-permute-start | bytes 1105928 | tf_op jit(solution)/shard_map/ppermute | solution.py:22
  64.9 5.6 %collective-permute-done.4 = bf16[480,384]{1,0:T(8,128)(2,1)S(1)} collective-permute-done((bf16[480,384]{1,0:T(8,128)(2,1)S(1)}, bf16[480,384]{1,0:T(8,128)(2,1)S(1)}, u32[]{:S(2)}, u32[]{:S(2)}) %collective-permute-start.4) | collective-permute-done | bytes 368672 | tf_op jit(solution)/shard_map/ppermute | solution.py:22
  70.6 5.1 %collective-permute-start.5 = (bf16[960,384]{1,0:T(8,128)(2,1)S(1)}, bf16[960,384]{1,0:T(8,128)(2,1)S(1)}, u32[]{:S(2)}, u32[]{:S(2)}) collective-permute-start(bf16[960,384]{1,0:T(8,128)(2,1)S(1)} %pad_maximum_fusion.2), channel_id=1, source_target_pairs={{0,4},{1,5},{2,6},{3,7},{4,0},{5,1},{6,2},{7,3},{8,12},{9,13},{10,... | collective-permute-start | bytes 2211848 | tf_op jit(solution)/shard_map/ppermute | solution.py:22
  75.6 15.8 %collective-permute-done.5 = bf16[960,384]{1,0:T(8,128)(2,1)S(1)} collective-permute-done((bf16[960,384]{1,0:T(8,128)(2,1)S(1)}, bf16[960,384]{1,0:T(8,128)(2,1)S(1)}, u32[]{:S(2)}, u32[]{:S(2)}) %collective-permute-start.5) | collective-permute-done | bytes 737312 | tf_op jit(solution)/shard_map/ppermute | solution.py:22
  91.4 1.4 pad_maximum_fusion
  92.9 2.8 %collective-permute-start.6 = (bf16[1920,384]{1,0:T(8,128)(2,1)}, bf16[1920,384]{1,0:T(8,128)(2,1)}, u32[]{:S(2)}, u32[]{:S(2)}) collective-permute-start(bf16[1920,384]{1,0:T(8,128)(2,1)} %pad_maximum_fusion), channel_id=1, source_target_pairs={{0,8},{1,9},{2,10},{3,11},{4,12},{5,13},{6,14},{7,15},{8,0},{9,1},... | collective-permute-start | bytes 4423688 | tf_op jit(solution)/shard_map/ppermute | solution.py:22
  95.6 0.4 convolution_convert_fusion.8
  96.0 0.7 copy-done.2
  96.8 0.7 fusion.156
  97.5 1.9 %fusion.155 = (f32[480]{0:T(512)S(1)}, f32[480,480]{0,1:T(8,128)S(1)}) fusion(bf16[480,384]{1,0:T(8,128)(2,1)} %copy-done.2, bf16[480,384]{1,0:T(8,128)(2,1)S(1)} %collective-permute-done.4, bf16[384,384]{1,0:T(8,128)(2,1)S(1)} %copy-done), kind=kOutput, calls=%fused_computation.206 | convolution fusion | flops 319149600 | bytes 1955712 | tf_op jit(solution)/shard_map/qc,kc->qk/dot_general | solution.py:83
  99.4 3.7 %multiply_reduce_fusion.1 = (f32[480]{0:T(512)S(1)}, f32[480,960]{1,0:T(8,128)}) fusion(bf16[480,384]{1,0:T(8,128)(2,1)} %copy-done.2, bf16[960,384]{1,0:T(8,128)(2,1)} %copy-done.3, bf16[384,384]{1,0:T(8,128)(2,1)S(1)} %copy-done), kind=kOutput, calls=%fused_computation.17 | convolution fusion | flops 638299648 | bytes 3245952 | tf_op jit(solution)/shard_map/qc,kc->qk/dot_general | solution.py:83
  103.1 55.2 %collective-permute-done.6 = bf16[1920,384]{1,0:T(8,128)(2,1)} collective-permute-done((bf16[1920,384]{1,0:T(8,128)(2,1)}, bf16[1920,384]{1,0:T(8,128)(2,1)}, u32[]{:S(2)}, u32[]{:S(2)}) %collective-permute-start.6) | collective-permute-done | bytes 1474592 | tf_op jit(solution)/shard_map/ppermute | solution.py:22
  158.4 5.3 %multiply_reduce_fusion = (f32[480]{0:T(512)S(1)}, f32[480,1920]{1,0:T(8,128)}) fusion(bf16[480,384]{1,0:T(8,128)(2,1)} %copy-done.2, bf16[1920,384]{1,0:T(8,128)(2,1)} %collective-permute-done.6, bf16[384,384]{1,0:T(8,128)(2,1)S(1)} %copy-done), kind=kOutput, calls=%fused_computation.4 | convolution fusion | flops 1276599808 | bytes 5826432 | tf_op jit(solution)/shard_map/qc,kc->qk/dot_general | solution.py:83
  163.7 2.0 %fusion.12 = f32[480]{0:T(512)S(1)} fusion(f32[480,960]{1,0:T(8,128)} %get-tuple-element.45, f32[480]{0:T(512)S(1)} %get-tuple-element.10), kind=kLoop, calls=%fused_computation.21 | loop fusion | flops 1381920 | bytes 1847040 | tf_op jit(solution)/shard_map/reduce_sum | solution.py:89
  165.8 2.8 %fusion.1 = f32[480]{0:T(512)S(1)} fusion(f32[480,1920]{1,0:T(8,128)} %get-tuple-element.43, f32[480]{0:T(512)S(1)} %get-tuple-element.9), kind=kLoop, calls=%fused_computation.5 | loop fusion | flops 2764320 | bytes 3690240 | tf_op jit(solution)/shard_map/reduce_sum | solution.py:89
  168.6 0.3 fusion.48
  168.9 2.7 %fusion.30 = f32[480,384]{1,0:T(8,128)} fusion(bf16[480,384]{1,0:T(8,128)(2,1)S(1)} %bitcast.172, bf16[384,384]{1,0:T(8,128)(2,1)} %param.16, f32[480,480]{0,1:T(8,128)S(1)} %get-tuple-element.49, f32[480]{0:T(512)S(1)} %get-tuple-element.41, f32[480]{0:T(512)S(1)} %get-tuple-element.8, f32[480]{0:T(512)S(1)} %get-tuple-element.40), kind=kOutput, calls=%fused_computation.48 | convolution fusion | flops 319518720 | bytes 2328192 | tf_op jit(solution)/shard_map/dot_general | solution.py:90
  171.6 3.9 %fusion.35 = f32[480,384]{1,0:T(8,128)} fusion(bf16[960,384]{1,0:T(8,128)(2,1)} %copy-done.3, bf16[384,384]{1,0:T(8,128)(2,1)} %param.16, f32[480,960]{1,0:T(8,128)} %get-tuple-element.45, f32[480]{0:T(512)S(1)} %get-tuple-element.10), kind=kOutput, calls=%fused_computation.53 | convolution fusion | flops 638760960 | bytes 3614592 | tf_op jit(solution)/shard_map/dot_general | solution.py:90
  175.4 5.4 %fusion.8 = f32[480,384]{1,0:T(8,128)} fusion(f32[480,1920]{1,0:T(8,128)} %get-tuple-element.43, f32[480]{0:T(512)S(1)} %get-tuple-element.9, bf16[1920,384]{1,0:T(8,128)(2,1)} %collective-permute-done.6, bf16[384,384]{1,0:T(8,128)(2,1)S(1)} %copy-done.7), kind=kOutput, calls=%fused_computation.18 | convolution fusion | flops 1277521920 | bytes 6195072 | tf_op jit(solution)/shard_map/dot_general | solution.py:90
  180.8 2.4 %fusion.44 = bf16[480,384]{1,0:T(8,128)(2,1)S(1)} fusion(f32[480,384]{1,0:T(8,128)} %fusion.8, f32[480,384]{1,0:T(8,128)} %fusion.35, f32[480,384]{1,0:T(8,128)} %fusion.30, bf16[480,384]{1,0:T(8,128)(2,1)S(1)} %collective-permute-done.4, bf16[384,384]{1,0:T(8,128)(2,1)S(1)} %copy-done.7, f32[480,480]{0,1:T(8,128)S(1)} %get-tuple-element.47, ...), kind=kOutput, calls=%fused_computation.67 | convolution fusion | flops 320440320 | bytes 4173312 | tf_op jit(solution)/shard_map/dot_general | solution.py:90
  183.2 0.4 fusion.157
  183.6 0.8 fusion.64
  (31 shorter events, 0.9 us)
Async XLA Ops:
  0.0 96.8 %copy-start = (bf16[384,384]{1,0:T(8,128)(2,1)S(1)}, bf16[384,384]{1,0:T(8,128)(2,1)}, u32[]{:S(2)}) copy-start(bf16[384,384]{1,0:T(8,128)(2,1)} %param.15) | copy-start | bytes 884740
  3.6 14.6 %collective-permute-start = (bf16[2,3,160,384]{3,2,1,0:T(8,128)(2,1)S(1)}, bf16[2,3,160,384]{3,2,1,0:T(8,128)(2,1)S(1)}, u32[]{:S(2)}, u32[]{:S(2)}) collective-permute-start(bf16[2,3,160,384]{3,2,1,0:T(8,128)(2,1)S(1)} %pad_maximum_fusion.1), channel_id=1, source_target_pairs={{0,1},{1,2},{2,3},{3,4},{4,5},{5,6},{6,7},{7,8},{8,9},{9,10},{10,1... | collective-permute-start | bytes 2211848 | tf_op jit(solution)/shard_map/ppermute | solution.py:10
  18.3 13.6 %collective-permute-start.1 = (bf16[2,3,160,384]{3,2,1,0:T(8,128)(2,1)S(1)}, bf16[2,3,160,384]{3,2,1,0:T(8,128)(2,1)S(1)}, u32[]{:S(2)}, u32[]{:S(2)}) collective-permute-start(bf16[2,3,160,384]{3,2,1,0:T(8,128)(2,1)S(1)} %collective-permute-done), channel_id=1, source_target_pairs={{0,1},{1,2},{2,3},{3,4},{4,5},{5,6},{6,7},{7,8},{8,9},{9,10},{10,1... | collective-permute-start | bytes 2211848 | tf_op jit(solution)/shard_map/ppermute | solution.py:10
  32.0 14.4 %collective-permute-start.2 = (bf16[3,1,160,384]{3,2,1,0:T(8,128)(2,1)S(1)}, bf16[3,1,160,384]{3,2,1,0:T(8,128)(2,1)S(1)}, u32[]{:S(2)}, u32[]{:S(2)}) collective-permute-start(bf16[3,1,160,384]{3,2,1,0:T(8,128)(2,1)S(1)} %get-tuple-element.38), channel_id=1, source_target_pairs={{0,2},{1,3},{2,4},{3,5},{4,6},{5,7},{6,8},{7,9},{8,10},{9,11},{10,... | collective-permute-start | bytes 1105928 | tf_op jit(solution)/shard_map/ppermute | solution.py:16
  33.3 13.1 %collective-permute-start.3 = (bf16[3,1,160,384]{3,2,1,0:T(8,128)(2,1)S(1)}, bf16[3,1,160,384]{3,2,1,0:T(8,128)(2,1)S(1)}, u32[]{:S(2)}, u32[]{:S(2)}) collective-permute-start(bf16[3,1,160,384]{3,2,1,0:T(8,128)(2,1)S(1)} %get-tuple-element.39), channel_id=1, source_target_pairs={{2,0},{3,1},{4,2},{5,3},{6,4},{7,5},{8,6},{9,7},{10,8},{11,9},{12,... | collective-permute-start | bytes 1105928 | tf_op jit(solution)/shard_map/ppermute | solution.py:16
  46.4 2.8 %slice-start = ((s8[7962624]{0:T(1024)(128)(4,1)}), s8[4194304]{0:T(1024)(128)(4,1)S(1)}, s32[]{:S(2)}) async-start(s8[7962624]{0:T(1024)(128)(4,1)} %bitcast.173), calls=%async_computation | async-start | bytes 8388608
  48.2 2.2 %slice-start.1 = ((s8[7962624]{0:T(1024)(128)(4,1)}), s8[3768320]{0:T(1024)(128)(4,1)S(1)}, s32[]{:S(2)}) async-start(s8[7962624]{0:T(1024)(128)(4,1)} %bitcast.173), calls=%async_computation.1 | async-start | bytes 7536640
  61.0 1.0 copy-start.1
  61.0 1.2 copy-start.6
  61.4 34.2 %copy-start.4 = (bf16[384,384]{1,0:T(8,128)(2,1)S(1)}, bf16[384,384]{1,0:T(8,128)(2,1)}, u32[]{:S(2)}) copy-start(bf16[384,384]{1,0:T(8,128)(2,1)} %param.14) | copy-start | bytes 884740
  62.4 8.1 %collective-permute-start.4 = (bf16[480,384]{1,0:T(8,128)(2,1)S(1)}, bf16[480,384]{1,0:T(8,128)(2,1)S(1)}, u32[]{:S(2)}, u32[]{:S(2)}) collective-permute-start(bf16[480,384]{1,0:T(8,128)(2,1)S(1)} %bitcast.167), channel_id=1, source_target_pairs={{0,2},{1,3},{2,0},{3,1},{4,6},{5,7},{6,4},{7,5},{8,10},{9,11},{10,... | collective-permute-start | bytes 1105928 | tf_op jit(solution)/shard_map/ppermute | solution.py:22
  70.6 20.9 %collective-permute-start.5 = (bf16[960,384]{1,0:T(8,128)(2,1)S(1)}, bf16[960,384]{1,0:T(8,128)(2,1)S(1)}, u32[]{:S(2)}, u32[]{:S(2)}) collective-permute-start(bf16[960,384]{1,0:T(8,128)(2,1)S(1)} %pad_maximum_fusion.2), channel_id=1, source_target_pairs={{0,4},{1,5},{2,6},{3,7},{4,0},{5,1},{6,2},{7,3},{8,12},{9,13},{10,... | collective-permute-start | bytes 2211848 | tf_op jit(solution)/shard_map/ppermute | solution.py:22
  91.4 4.2 %copy-start.3 = (bf16[960,384]{1,0:T(8,128)(2,1)}, bf16[960,384]{1,0:T(8,128)(2,1)S(1)}, u32[]{:S(2)}) copy-start(bf16[960,384]{1,0:T(8,128)(2,1)S(1)} %collective-permute-done.5) | copy-start | bytes 2211844
  92.9 65.5 %collective-permute-start.6 = (bf16[1920,384]{1,0:T(8,128)(2,1)}, bf16[1920,384]{1,0:T(8,128)(2,1)}, u32[]{:S(2)}, u32[]{:S(2)}) collective-permute-start(bf16[1920,384]{1,0:T(8,128)(2,1)} %pad_maximum_fusion), channel_id=1, source_target_pairs={{0,8},{1,9},{2,10},{3,11},{4,12},{5,13},{6,14},{7,15},{8,0},{9,1},... | collective-permute-start | bytes 4423688 | tf_op jit(solution)/shard_map/ppermute | solution.py:22
  96.0 0.7 copy-start.2
  171.5 3.9 %copy-start.7 = (bf16[384,384]{1,0:T(8,128)(2,1)S(1)}, bf16[384,384]{1,0:T(8,128)(2,1)}, u32[]{:S(2)}) copy-start(bf16[384,384]{1,0:T(8,128)(2,1)} %param.16) | copy-start | bytes 884740
  180.8 2.4 %copy-start.5 = (bf16[384,384]{1,0:T(8,128)(2,1)S(1)}, bf16[384,384]{1,0:T(8,128)(2,1)}, u32[]{:S(2)}) copy-start(bf16[384,384]{1,0:T(8,128)(2,1)} %param.17) | copy-start | bytes 884740
where the time goes:
time: 185 us; the launch traced here: 184 us
  waiting for transfers between devices  112 us (61%)
  matrix products  40 us (22%)
  other arithmetic  15 us (8%)
  starting transfers between devices  13.5 us (7%)
  local copies, waits for them, and re-layouts  3.47 us (2%)
    ppermute x3, waiting for transfers between devices, swapped(): return lax.ppermute(value, axis, pairs)  76.6 us
    ppermute x2, waiting for transfers between devices, from_behind(): return lax.ppermute(value, axis, pairs)  26.4 us
    dot_general x4, matrix products, absorb(): jnp.dot(weights.astype(jnp.bfloat16), value_part, preferred_element_type=...  14.3 us
    dot_general x27, matrix products, body(): jnp.dot(window.reshape(-1, channels), conv_kernel[time_tap, row_tap, col_...  13.2 us
    dot_general x4, matrix products, absorb(): jnp.einsum('qc,kc->qk', queries, key_part, preferred_element_type=jnp.flo...  11.7 us
    ppermute x3, starting transfers between devices, swapped(): return lax.ppermute(value, axis, pairs)  10.4 us
    ppermute x2, waiting for transfers between devices, passed_along(): return lax.ppermute(block, axis, route)  9.1 us
    reduce_sum x3, other arithmetic, absorb(): weight_sum = weight_sum * rescale + jnp.sum(weights, axis=-1)  5.12 us
  transfers between devices with their start and end apart: 7, of which 6 were waited for; matrix products, arithmetic and copies ran while one was open for 6% of the time, Pallas kernels for 0%

commit v1 on v0

v1 whole, which is shorter than its diff:
```python
import functools

import jax
import jax.numpy as jnp
from jax import lax
from jax.experimental import pallas as pl
from jax.experimental.pallas import tpu as pltpu
from jax.sharding import PartitionSpec as P


def from_behind(value, axis, steps):
    count = lax.axis_size(axis)
    pairs = [(source, (source + steps) % count) for source in range(count)]
    return lax.ppermute(value, axis, pairs)


def passed_along(block, axis, distance):
    devices = range(lax.axis_size(axis))
    route = [(i - distance, i) for i in devices if i - distance in devices]
    return lax.ppermute(block, axis, route)


def rms_scale(inputs, scale_gain):
    floats = inputs.astype(jnp.float32)
    return (
        floats * lax.rsqrt(jnp.mean(floats * floats, axis=-1, keepdims=True) + 1e-06) * scale_gain
    )


def dot32(a, b):
    return jnp.dot(a, b, preferred_element_type=jnp.float32)


def ring_tile(place, row_tiles):
    half = row_tiles // 2
    return jnp.where(place < half, 2 * place, 2 * (row_tiles - 1 - place) + 1)


def attend_kernel(
    frames,
    row_tiles,
    pieces,
    normed_ref,
    residual_ref,
    wq_ref,
    wk_ref,
    wv_ref,
    wo_ref,
    out_ref,
    held,
    queries,
    highest,
    total,
    acc,
    send_sem,
    recv_sem,
):
    positions, channels = normed_ref.shape
    half = row_tiles // 2
    piece = positions // pieces
    scale = float(channels) ** (-0.5)
    me = lax.axis_index("tile")
    frame = lax.rem(me, frames)
    tile = lax.div(me, frames)
    place = jnp.where(
        lax.rem(tile, 2) == 0, lax.div(tile, 2), row_tiles - 1 - lax.div(tile, 2)
    )
    right = ring_tile(lax.rem(place + 1, row_tiles), row_tiles) * frames + frame
    left = ring_tile(lax.rem(place + row_tiles - 1, row_tiles), row_tiles) * frames + frame

    barrier = pltpu.get_barrier_semaphore()
    for neighbour in (left, right):
        pl.semaphore_signal(
            barrier, inc=1, device_id={"tile": neighbour}, device_id_type=pl.DeviceIdType.MESH
        )
    held[0] = normed_ref[...]
    pl.semaphore_wait(barrier, 2)

    def copy(way, step, part):
        if way == 0:
            source, target, peer = step - 1, step, right
        else:
            source, target, peer = (
                lax.rem(row_tiles - step + 1, row_tiles),
                row_tiles - step,
                left,
            )
        rows = pl.ds(pl.multiple_of(part * piece, piece), piece)
        return pltpu.make_async_remote_copy(
            src_ref=held.at[source, rows],
            dst_ref=held.at[target, rows],
            send_sem=send_sem.at[way, step, part],
            recv_sem=recv_sem.at[way, step, part],
            device_id={"tile": peer},
            device_id_type=pl.DeviceIdType.MESH,
        )

    def runs(way, step, part):
        last = (part < pieces // 2) if way == 0 else (part >= pieces // 2)
        return jnp.logical_or(step < half, jnp.logical_and(step == half, last))

    for part in range(pieces):
        for way in range(2):
            copy(way, 1, part).start()

    queries[...] = dot32(normed_ref[...], wq_ref[...]).astype(jnp.bfloat16)
    highest[...] = jnp.full(highest.shape, -1e30, jnp.float32)
    total[...] = jnp.zeros(total.shape, jnp.float32)
    acc[...] = jnp.zeros(acc.shape, jnp.float32)

    def absorb(slot, part):
        rows = pl.ds(pl.multiple_of(part * piece, piece), piece)
        block = held[slot, rows]
        keys = dot32(block, wk_ref[...]).astype(jnp.bfloat16)
        values = dot32(block, wv_ref[...]).astype(jnp.bfloat16)
        scores = (
            lax.dot_general(
                queries[...], keys, (((1,), (1,)), ((), ())), preferred_element_type=jnp.float32
            )
            * scale
        )
        before = highest[...]
        now = jnp.maximum(before, jnp.max(scores, axis=-1, keepdims=True))
        rescale = jnp.exp(before - now)
        weights = jnp.exp(scores - now)
        highest[...] = now
        total[...] = total[...] * rescale + jnp.sum(weights, axis=-1, keepdims=True)
        acc[...] = acc[...] * rescale + dot32(weights.astype(jnp.bfloat16), values)

    def own(part, carry):
        absorb(0, part)
        return carry

    lax.fori_loop(0, pieces, own, 0)

    def visit(index, carry):
        step = lax.div(index, pieces) + 1
        part = lax.rem(index, pieces)
        for way in range(2):

            @pl.when(runs(way, step, part))
            def _(way=way):
                copy(way, step, part).wait_recv()

            @pl.when(runs(way, step + 1, part))
            def _(way=way):
                copy(way, step + 1, part).start()

        def one(way, carry):
            absorb(jnp.where(way == 0, step, row_tiles - step), part)
            return carry

        lax.fori_loop(0, jnp.where(step == half, 1, 2), one, 0)
        return carry

    lax.fori_loop(0, half * pieces, visit, 0)

    attended = (acc[...] / total[...]).astype(jnp.bfloat16)
    out_ref[...] = (
        residual_ref[...].astype(jnp.float32) + dot32(attended, wo_ref[...])
    ).astype(jnp.bfloat16)

    def finish(index, carry):
        step = lax.div(index, pieces) + 1
        part = lax.rem(index, pieces)
        for way in range(2):

            @pl.when(runs(way, step, part))
            def _(way=way):
                copy(way, step, part).wait_send()

        return carry

    lax.fori_loop(0, half * pieces, finish, 0)


def attend(normed, residual, weights, frames, row_tiles, pieces=2):
    positions, channels = normed.shape
    half = row_tiles // 2
    return pl.pallas_call(
        functools.partial(attend_kernel, frames, row_tiles, pieces),
        out_shape=jax.ShapeDtypeStruct((positions, channels), jnp.bfloat16),
        in_specs=[pl.BlockSpec(memory_space=pltpu.VMEM)] * 6,
        out_specs=pl.BlockSpec(memory_space=pltpu.VMEM),
        scratch_shapes=[
            pltpu.VMEM((row_tiles, positions, channels), jnp.bfloat16),
            pltpu.VMEM((positions, channels), jnp.bfloat16),
            pltpu.VMEM((positions, 1), jnp.float32),
            pltpu.VMEM((positions, 1), jnp.float32),
            pltpu.VMEM((positions, channels), jnp.float32),
            pltpu.SemaphoreType.DMA((2, half + 1, pieces)),
            pltpu.SemaphoreType.DMA((2, half + 1, pieces)),
        ],
        compiler_params=pltpu.CompilerParams(
            collective_id=0, has_side_effects=True, vmem_limit_bytes=40 * 2**20
        ),
    )(normed, residual, *weights)


def body(
    video_latent, conv_cache, norm_gain, conv_kernel, attend_gain, w_query, w_key, w_value, w_output
):
    rows_local, cols_all, channels = video_latent.shape
    tiles = lax.axis_size("tile")
    row_tiles = min(16, tiles // 2)
    frames = tiles // row_tiles
    position = lax.axis_index("tile")
    time_group = position % frames
    activated = jax.nn.silu(rms_scale(video_latent, norm_gain)).astype(jnp.bfloat16)
    frame_pair = jnp.stack([activated, conv_cache])
    before_one = from_behind(frame_pair, "tile", 1)
    before_two = from_behind(before_one, "tile", 1)
    frame_one = jnp.where(time_group >= 1, before_one[0], before_one[1])
    frame_two = jnp.where(time_group >= 2, before_two[0], before_two[1])
    stacked = jnp.stack([frame_two, frame_one, frame_pair[0]])
    rim_above = passed_along(stacked[:, -1:], "tile", frames)
    rim_below = passed_along(stacked[:, :1], "tile", -frames)
    stacked = jnp.concatenate([rim_above, stacked, rim_below], axis=1)
    padded = jnp.pad(stacked, ((0, 0), (0, 0), (1, 1), (0, 0)))
    summed = jnp.zeros((rows_local * cols_all, channels), jnp.float32)
    for time_tap in range(3):
        for row_tap in range(3):
            for col_tap in range(3):
                window = padded[
                    time_tap, row_tap : row_tap + rows_local, col_tap : col_tap + cols_all
                ]
                summed = summed + dot32(
                    window.reshape(-1, channels), conv_kernel[time_tap, row_tap, col_tap]
                )
    residual = (video_latent.astype(jnp.float32) + summed.reshape(video_latent.shape)).astype(
        jnp.bfloat16
    )
    normed = rms_scale(residual, attend_gain).astype(jnp.bfloat16)
    result = attend(
        normed.reshape(-1, channels),
        residual.reshape(-1, channels),
        (w_query, w_key, w_value, w_output),
        frames,
        row_tiles,
    )
    return result.reshape(video_latent.shape)


def solution(mesh):
    placed = (
        P(("groups", "tile"), None, None),
        P(("groups", "tile"), None, None),
        P(),
        P(),
        P(),
        P(),
        P(),
        P(),
        P(),
    )
    return jax.shard_map(
        body,
        mesh=mesh,
        in_specs=placed,
        out_specs=P(("groups", "tile"), None, None),
        check_vma=False,
    )
```

time: 185 us -> 98.7 us (0.53)
  waiting for transfers between devices: 112 us -> 35.5 us
  Pallas kernels: 0 us -> 36.2 us
  matrix products: 40 us -> 12.9 us
  starting transfers between devices: 13.5 us -> 3.11 us
  other arithmetic: 15 us -> 7.3 us
    ppermute x3 -> x0, waiting for transfers between devices: 76.6 us -> none  [swapped(): return lax.ppermute(value, axis, pairs)]
    pallas_call x0 -> x1, Pallas kernels: none -> 36.2 us  [attend(): pl.pallas_call(functools.partial(attend_kernel, frames, row_tiles, pieces...]
    dot_general x37 -> x27, matrix products: 40 us -> 12.9 us  [dot32(): return jnp.dot(a, b, preferred_element_type=jnp.float32)]
    ppermute x3 -> x0, starting transfers between devices: 10.4 us -> none  [swapped(): return lax.ppermute(value, axis, pairs)]
    reduce_sum x3 -> x0, other arithmetic: 5.12 us -> none  [absorb(): weight_sum = weight_sum * rescale + jnp.sum(weights, axis=-1)]
  transfers between devices with their start and end apart: 7 -> 4, of which waited for: 6 -> 3; matrix products, arithmetic and copies ran while one was open for 6% -> 4% of each run, Pallas kernels for 0% -> 0%
where the time goes in v1:
time: 98.7 us; the launch traced here: 98.3 us
  Pallas kernels  36.2 us (37%)
  waiting for transfers between devices  35.5 us (36%)
  matrix products  12.9 us (13%)
  other arithmetic  7.3 us (7%)
  starting transfers between devices  3.11 us (3%)
  local copies, waits for them, and re-layouts  2.83 us (3%)
    pallas_call x1, Pallas kernels, attend(): pl.pallas_call(functools.partial(attend_kernel, frames, row_tiles, pieces...  36.2 us
    ppermute x2, waiting for transfers between devices, from_behind(): return lax.ppermute(value, axis, pairs)  26.4 us
    dot_general x27, matrix products, dot32(): return jnp.dot(a, b, preferred_element_type=jnp.float32)  12.9 us
    ppermute x2, waiting for transfers between devices, passed_along(): return lax.ppermute(block, axis, route)  9.09 us
    ppermute x2, starting transfers between devices, passed_along(): return lax.ppermute(block, axis, route)  2.6 us
    another operation x2, other arithmetic, body(): frame_pair = jnp.stack([activated, conv_cache])  2.37 us
  transfers between devices with their start and end apart: 4, of which 3 were waited for; matrix products, arithmetic and copies ran while one was open for 4% of the time, Pallas kernels for 0%

profile of v1, /device:TPU:0, one launch (start us, length us, event | category | flops | bytes accessed | tf_op | source)
XLA Modules:
  0.0 98.3 jit_solution(11963920880671458551)
XLA Ops:
  0.0 1.2 %fusion.30 = f32[3,160]{1,0:T(4,128)S(1)} fusion(bf16[3,160,384]{2,1,0:T(8,128)(2,1)} %param.9), kind=kLoop, calls=%fused_computation.41 | loop fusion | flops 552480 | bytes 370560 | tf_op jit(solution)/shard_map/reduce_sum | solution.py:26
  1.2 1.3 %fusion.147 = bf16[1,3,160,384]{3,2,1,0:T(8,128)(2,1)S(1)} fusion(f32[384]{0:T(512)} %param.11, f32[3,160]{1,0:T(4,128)S(1)} %add_rsqrt_fusion.1, bf16[3,160,384]{2,1,0:T(8,128)(2,1)} %param.9), kind=kLoop, calls=%fused_computation.148 | loop fusion | flops 1474560 | bytes 740736 | tf_op jit(solution)/shard_map/stack | solution.py:210
  2.5 1.1 %pad_maximum_fusion = bf16[2,3,160,384]{3,2,1,0:T(8,128)(2,1)S(1)} fusion(bf16[1,3,160,384]{3,2,1,0:T(8,128)(2,1)} %bitcast.175, bf16[1,3,160,384]{3,2,1,0:T(8,128)(2,1)S(1)} %fusion.147), kind=kLoop, calls=%fused_computation.50 | loop fusion | flops 368640 | bytes 1474560 | tf_op jit(solution)/shard_map/stack | solution.py:210
  3.6 0.5 collective-permute-start
  4.1 14.1 %collective-permute-done = bf16[2,3,160,384]{3,2,1,0:T(8,128)(2,1)S(1)} collective-permute-done((bf16[2,3,160,384]{3,2,1,0:T(8,128)(2,1)S(1)}, bf16[2,3,160,384]{3,2,1,0:T(8,128)(2,1)S(1)}, u32[]{:S(2)}, u32[]{:S(2)}) %collective-permute-start) | collective-permute-done | bytes 737312 | tf_op jit(solution)/shard_map/ppermute | solution.py:14
  18.2 0.0 collective-permute-start.1
  18.2 1.3 %fusion.37 = bf16[3,160,384]{2,1,0:T(8,128)(2,1)S(1)} fusion(bf16[3,160,384]{2,1,0:T(8,128)(2,1)} %param.9, f32[384]{0:T(512)} %param.11, f32[3,160]{1,0:T(4,128)S(1)} %add_rsqrt_fusion.1), kind=kLoop, calls=%fused_computation.48 | loop fusion | flops 1474560 | bytes 740736 | tf_op jit(solution)/shard_map/convert_element_type | solution.py:209
  19.6 12.2 %collective-permute-done.1 = bf16[2,3,160,384]{3,2,1,0:T(8,128)(2,1)S(1)} collective-permute-done((bf16[2,3,160,384]{3,2,1,0:T(8,128)(2,1)S(1)}, bf16[2,3,160,384]{3,2,1,0:T(8,128)(2,1)S(1)}, u32[]{:S(2)}, u32[]{:S(2)}) %collective-permute-start.1) | collective-permute-done | bytes 737312 | tf_op jit(solution)/shard_map/ppermute | solution.py:14
  31.9 0.1 pad_maximum_fusion.13
  32.0 1.3 %collective-permute-start.2 = (bf16[3,1,160,384]{3,2,1,0:T(8,128)(2,1)S(1)}, bf16[3,1,160,384]{3,2,1,0:T(8,128)(2,1)S(1)}, u32[]{:S(2)}, u32[]{:S(2)}) collective-permute-start(bf16[3,1,160,384]{3,2,1,0:T(8,128)(2,1)S(1)} %get-tuple-element.31), channel_id=1, source_target_pairs={{0,2},{1,3},{2,4},{3,5},{4,6},{5,7},{6,8},{7,9},{8,10},{9,11},{10,... | collective-permute-start | bytes 1105928 | tf_op jit(solution)/shard_map/ppermute | solution.py:20
  33.3 1.3 %collective-permute-start.3 = (bf16[3,1,160,384]{3,2,1,0:T(8,128)(2,1)S(1)}, bf16[3,1,160,384]{3,2,1,0:T(8,128)(2,1)S(1)}, u32[]{:S(2)}, u32[]{:S(2)}) collective-permute-start(bf16[3,1,160,384]{3,2,1,0:T(8,128)(2,1)S(1)} %get-tuple-element.32), channel_id=1, source_target_pairs={{2,0},{3,1},{4,2},{5,3},{6,4},{7,5},{8,6},{9,7},{10,8},{11,9},{12,... | collective-permute-start | bytes 1105928 | tf_op jit(solution)/shard_map/ppermute | solution.py:20
  34.6 1.3 %fusion.46 = f32[480,384]{1,0:T(8,128)S(1)} fusion(bf16[480,384]{1,0:T(8,128)(2,1)S(1)} %bitcast.174, bf16[3,3,3,384,384]{4,3,2,1,0:T(8,128)(2,1)} %param.12), kind=kOutput, calls=%fused_computation.73 | convolution fusion | flops 141557760 | bytes 1400832 | tf_op jit(solution)/shard_map/dot_general | solution.py:31
  35.9 1.3 %fusion.64 = f32[480,384]{1,0:T(8,128)S(1)} fusion(bf16[480,384]{1,0:T(8,128)(2,1)S(1)} %bitcast.145, bf16[3,3,3,384,384]{4,3,2,1,0:T(8,128)(2,1)} %param.12), kind=kOutput, calls=%fused_computation.91 | convolution fusion | flops 141557760 | bytes 1400832 | tf_op jit(solution)/shard_map/dot_general | solution.py:31
  37.3 0.0 slice-start
  37.3 9.1 %collective-permute-done.2 = bf16[3,1,160,384]{3,2,1,0:T(8,128)(2,1)S(1)} collective-permute-done((bf16[3,1,160,384]{3,2,1,0:T(8,128)(2,1)S(1)}, bf16[3,1,160,384]{3,2,1,0:T(8,128)(2,1)S(1)}, u32[]{:S(2)}, u32[]{:S(2)}) %collective-permute-start.2) | collective-permute-done | bytes 368672 | tf_op jit(solution)/shard_map/ppermute | solution.py:20
  46.4 0.0 collective-permute-done.3
  46.4 1.5 %select_maximum_fusion = bf16[3,5,162,384]{3,2,1,0:T(8,128)(2,1)S(1)} fusion(bf16[3,1,160,384]{3,2,1,0:T(8,128)(2,1)S(1)} %collective-permute-done.3, bf16[3,1,160,384]{3,2,1,0:T(8,128)(2,1)S(1)} %collective-permute-done.2, bf16[1,3,160,384]{3,2,1,0:T(8,128)(2,1)S(1)} %fusion.147, bf16[1,3,160,384]{3,2,1,0:T(8,128)(2,1)S(1)} %slice_select_fusion, ...), kind=kLoop, calls=%fused_computation.3 | loop fusion | flops 16796160 | bytes 3709440 | tf_op jit(solution)/shard_map/concatenate | solution.py:218
  47.9 0.0 slice-start.1
  48.0 1.1 %fusion.119 = (bf16[1,3,160,384]{3,2,1,0:T(8,128)(2,1)S(1)}, bf16[1,3,160,384]{3,2,1,0:T(8,128)(2,1)S(1)}, bf16[1,3,160,384]{3,2,1,0:T(8,128)(2,1)S(1)}, bf16[1,...) fusion(bf16[3,5,162,384]{3,2,1,0:T(8,128)(2,1)S(1)} %select_max, ...), kind=kLoop, calls=%fused_computation.147 | loop fusion | bytes 13271040 | tf_op jit(solution)/shard_map/slice | solution.py:224
  49.1 0.0 slice-done
  49.1 0.9 slice-done.1
  50.0 0.4 fusion.48
  50.4 0.4 fusion.50
  50.8 0.4 fusion.54
  51.2 0.4 fusion.56
  51.6 0.4 fusion.60
  51.9 0.4 fusion.62
  52.3 0.4 fusion.66
  52.7 0.4 fusion.68
  53.1 0.4 fusion.72
  53.5 0.4 fusion.74
  53.9 0.4 fusion.78
  54.3 0.4 fusion.80
  54.6 0.4 fusion.83
  55.0 0.4 fusion.85
  55.4 0.4 fusion.89
  55.8 0.2 pad_maximum_fusion.10
  56.0 0.4 fusion.52
  56.4 0.2 pad_maximum_fusion.9
  56.6 0.4 fusion.58
  56.9 0.4 fusion.70
  57.3 0.4 fusion.76
  57.7 0.4 fusion.87
  58.1 0.4 fusion.39
  58.5 0.4 fusion.43
  58.9 0.4 fusion.41
  59.3 0.0 copy-start.4
  59.3 0.0 copy-start.5
  59.3 0.0 copy-start
  59.3 0.0 copy-start.1
  59.3 0.0 copy-start.2
  59.3 0.0 copy-start.3
  59.3 1.1 %fusion.26 = f32[480,384]{1,0:T(8,128)S(1)} fusion(f32[480,384]{1,0:T(8,128)S(1)} %fusion.46, f32[480,384]{1,0:T(8,128)S(1)} %fusion.48, f32[480,384]{1,0:T(8,128)S(1)} %fusion.50, f32[480,384]{1,0:T(8,128)S(1)} %fusion.52, f32[480,384]{1,0:T(8,128)S(1)} %fusion.54, f32[480,384]{1,0:T(8,128)S(1)} %fusion.56, f32[480,384]{1,0:T(8,128)S(1)} %fusion.58, ...), kind=kOutput, calls=%fused_computation.32 | convolution fusion | flops 145612800 | bytes 17620992 | tf_op jit(solution)/shard_map/dot_general | solution.py:31
  60.5 0.4 fusion.19
  60.9 0.0 copy-done.4
  60.9 0.2 fusion.27
  61.1 0.0 copy-done.5
  61.1 0.2 fusion.29
  61.3 0.0 copy-done
  61.3 0.0 copy-done.1
  61.3 0.0 copy-done.2
  61.3 0.0 copy-done.3
  61.3 36.2 %shard_map.91 = bf16[480,384]{1,0:T(8,128)(2,1)S(1)} custom-call(bf16[480,384]{1,0:T(8,128)(2,1)S(1)} %bitcast.143, bf16[480,384]{1,0:T(8,128)(2,1)S(1)} %bitcast.142, bf16[384,384]{1,0:T(8,128)(2,1)S(1)} %copy-done, bf16[384,384]{1,0:T(8,128)(2,1)S(1)} %copy-done.1, bf16[384,384]{1,0:T(8,128)(2,1)S(1)} %copy-done.2, bf16[384,384]{1,0:T(8,128)(2,1)S(1)} %copy-done.3), custom_call_target="tpu_custom_call" | custom-call | tf_op jit(solution)/shard_map/pallas_call | solution.py:180
  97.6 0.7 copy.11
  (5 shorter events, 0.1 us)
Async XLA Ops:
  3.6 14.6 %collective-permute-start = (bf16[2,3,160,384]{3,2,1,0:T(8,128)(2,1)S(1)}, bf16[2,3,160,384]{3,2,1,0:T(8,128)(2,1)S(1)}, u32[]{:S(2)}, u32[]{:S(2)}) collective-permute-start(bf16[2,3,160,384]{3,2,1,0:T(8,128)(2,1)S(1)} %pad_maximum_fusion), channel_id=1, source_target_pairs={{0,1},{1,2},{2,3},{3,4},{4,5},{5,6},{6,7},{7,8},{8,9},{9,10},{10,1... | collective-permute-start | bytes 2211848 | tf_op jit(solution)/shard_map/ppermute | solution.py:14
  18.2 13.6 %collective-permute-start.1 = (bf16[2,3,160,384]{3,2,1,0:T(8,128)(2,1)S(1)}, bf16[2,3,160,384]{3,2,1,0:T(8,128)(2,1)S(1)}, u32[]{:S(2)}, u32[]{:S(2)}) collective-permute-start(bf16[2,3,160,384]{3,2,1,0:T(8,128)(2,1)S(1)} %collective-permute-done), channel_id=1, source_target_pairs={{0,1},{1,2},{2,3},{3,4},{4,5},{5,6},{6,7},{7,8},{8,9},{9,10},{10,1... | collective-permute-start | bytes 2211848 | tf_op jit(solution)/shard_map/ppermute | solution.py:14
  32.0 14.4 %collective-permute-start.2 = (bf16[3,1,160,384]{3,2,1,0:T(8,128)(2,1)S(1)}, bf16[3,1,160,384]{3,2,1,0:T(8,128)(2,1)S(1)}, u32[]{:S(2)}, u32[]{:S(2)}) collective-permute-start(bf16[3,1,160,384]{3,2,1,0:T(8,128)(2,1)S(1)} %get-tuple-element.31), channel_id=1, source_target_pairs={{0,2},{1,3},{2,4},{3,5},{4,6},{5,7},{6,8},{7,9},{8,10},{9,11},{10,... | collective-permute-start | bytes 1105928 | tf_op jit(solution)/shard_map/ppermute | solution.py:20
  33.3 13.1 %collective-permute-start.3 = (bf16[3,1,160,384]{3,2,1,0:T(8,128)(2,1)S(1)}, bf16[3,1,160,384]{3,2,1,0:T(8,128)(2,1)S(1)}, u32[]{:S(2)}, u32[]{:S(2)}) collective-permute-start(bf16[3,1,160,384]{3,2,1,0:T(8,128)(2,1)S(1)} %get-tuple-element.32), channel_id=1, source_target_pairs={{2,0},{3,1},{4,2},{5,3},{6,4},{7,5},{8,6},{9,7},{10,8},{11,9},{12,... | collective-permute-start | bytes 1105928 | tf_op jit(solution)/shard_map/ppermute | solution.py:20
  37.3 11.8 %slice-start = ((s8[7962624]{0:T(1024)(128)(4,1)}), s8[4194304]{0:T(1024)(128)(4,1)S(1)}, s32[]{:S(2)}) async-start(s8[7962624]{0:T(1024)(128)(4,1)} %bitcast.147), calls=%async_computation | async-start | bytes 8388608
  47.9 2.1 %slice-start.1 = ((s8[7962624]{0:T(1024)(128)(4,1)}), s8[3768320]{0:T(1024)(128)(4,1)S(1)}, s32[]{:S(2)}) async-start(s8[7962624]{0:T(1024)(128)(4,1)} %bitcast.147), calls=%async_computation.1 | async-start | bytes 7536640
  59.3 1.6 %copy-start.4 = (bf16[3,160,384]{2,1,0:T(8,128)(2,1)S(1)}, bf16[3,160,384]{2,1,0:T(8,128)(2,1)}, u32[]{:S(2)}) copy-start(bf16[3,160,384]{2,1,0:T(8,128)(2,1)} %param.9) | copy-start | bytes 1105924
  59.3 1.9 %copy-start.5 = (f32[384]{0:T(512)S(1)}, f32[384]{0:T(512)}, u32[]{:S(2)}) copy-start(f32[384]{0:T(512)} %param.13) | copy-start | bytes 4612
  59.3 2.0 %copy-start = (bf16[384,384]{1,0:T(8,128)(2,1)S(1)}, bf16[384,384]{1,0:T(8,128)(2,1)}, u32[]{:S(2)}) copy-start(bf16[384,384]{1,0:T(8,128)(2,1)} %wq_ref.1) | copy-start | bytes 884740
  59.3 2.0 %copy-start.1 = (bf16[384,384]{1,0:T(8,128)(2,1)S(1)}, bf16[384,384]{1,0:T(8,128)(2,1)}, u32[]{:S(2)}) copy-start(bf16[384,384]{1,0:T(8,128)(2,1)} %wk_ref.1) | copy-start | bytes 884740
  59.3 2.0 %copy-start.2 = (bf16[384,384]{1,0:T(8,128)(2,1)S(1)}, bf16[384,384]{1,0:T(8,128)(2,1)}, u32[]{:S(2)}) copy-start(bf16[384,384]{1,0:T(8,128)(2,1)} %wv_ref.1) | copy-start | bytes 884740
  59.3 2.0 %copy-start.3 = (bf16[384,384]{1,0:T(8,128)(2,1)S(1)}, bf16[384,384]{1,0:T(8,128)(2,1)}, u32[]{:S(2)}) copy-start(bf16[384,384]{1,0:T(8,128)(2,1)} %wo_ref.1) | copy-start | bytes 884740

commit v2 on v1

--- a/solution.py
+++ b/solution.py
@@ -36,11 +36,25 @@
     return jnp.where(place < half, 2 * place, 2 * (row_tiles - 1 - place) + 1)
 
 
-def attend_kernel(
-    frames,
+MESH = pl.DeviceIdType.MESH
+
+
+def place_of(tile, row_tiles):
+    return jnp.where(lax.rem(tile, 2) == 0, lax.div(tile, 2), row_tiles - 1 - lax.div(tile, 2))
+
+
+def ring_neighbours(tile, row_tiles):
+    place = place_of(tile, row_tiles)
+    right = ring_tile(lax.rem(place + 1, row_tiles), row_tiles)
+    left = ring_tile(lax.rem(place + row_tiles - 1, row_tiles), row_tiles)
+    return left, right
+
+
+def attend_ring(
     row_tiles,
     pieces,
-    normed_ref,
+    left,
+    right,
     residual_ref,
     wq_ref,
     wk_ref,
@@ -55,26 +69,10 @@
     send_sem,
     recv_sem,
 ):
-    positions, channels = normed_ref.shape
+    positions, channels = residual_ref.shape
     half = row_tiles // 2
     piece = positions // pieces
     scale = float(channels) ** (-0.5)
-    me = lax.axis_index("tile")
-    frame = lax.rem(me, frames)
-    tile = lax.div(me, frames)
-    place = jnp.where(
-        lax.rem(tile, 2) == 0, lax.div(tile, 2), row_tiles - 1 - lax.div(tile, 2)
-    )
-    right = ring_tile(lax.rem(place + 1, row_tiles), row_tiles) * frames + frame
-    left = ring_tile(lax.rem(place + row_tiles - 1, row_tiles), row_tiles) * frames + frame
-
-    barrier = pltpu.get_barrier_semaphore()
-    for neighbour in (left, right):
-        pl.semaphore_signal(
-            barrier, inc=1, device_id={"tile": neighbour}, device_id_type=pl.DeviceIdType.MESH
-        )
-    held[0] = normed_ref[...]
-    pl.semaphore_wait(barrier, 2)
 
     def copy(way, step, part):
         if way == 0:
@@ -103,7 +101,7 @@
         for way in range(2):
             copy(way, 1, part).start()
 
-    queries[...] = dot32(normed_ref[...], wq_ref[...]).astype(jnp.bfloat16)
+    queries[...] = dot32(held[0], wq_ref[...]).astype(jnp.bfloat16)
     highest[...] = jnp.full(highest.shape, -1e30, jnp.float32)
     total[...] = jnp.zeros(total.shape, jnp.float32)
     acc[...] = jnp.zeros(acc.shape, jnp.float32)
@@ -174,27 +172,330 @@
     lax.fori_loop(0, half * pieces, finish, 0)
 
 
+def attend_kernel(
+    frames, row_tiles, pieces, normed_ref, residual_ref, wq, wk, wv, wo, out_ref, held, *scratch
+):
+    me = lax.axis_index("tile")
+    frame = lax.rem(me, frames)
+    left, right = ring_neighbours(lax.div(me, frames), row_tiles)
+    left, right = left * frames + frame, right * frames + frame
+    barrier = pltpu.get_barrier_semaphore()
+    for neighbour in (left, right):
+        pl.semaphore_signal(barrier, inc=1, device_id={"tile": neighbour}, device_id_type=MESH)
+    held[0] = normed_ref[...]
+    pl.semaphore_wait(barrier, 2)
+    attend_ring(
+        row_tiles, pieces, left, right, residual_ref, wq, wk, wv, wo, out_ref, held, *scratch
+    )
+
+
+def ring_scratch(row_tiles, pieces, positions, channels):
+    half = row_tiles // 2
+    return [
+        pltpu.VMEM((row_tiles, positions, channels), jnp.bfloat16),
+        pltpu.VMEM((positions, channels), jnp.bfloat16),
+        pltpu.VMEM((positions, 1), jnp.float32),
+        pltpu.VMEM((positions, 1), jnp.float32),
+        pltpu.VMEM((positions, channels), jnp.float32),
+        pltpu.SemaphoreType.DMA((2, half + 1, pieces)),
+        pltpu.SemaphoreType.DMA((2, half + 1, pieces)),
+    ]
+
+
 def attend(normed, residual, weights, frames, row_tiles, pieces=2):
     positions, channels = normed.shape
-    half = row_tiles // 2
     return pl.pallas_call(
         functools.partial(attend_kernel, frames, row_tiles, pieces),
         out_shape=jax.ShapeDtypeStruct((positions, channels), jnp.bfloat16),
         in_specs=[pl.BlockSpec(memory_space=pltpu.VMEM)] * 6,
         out_specs=pl.BlockSpec(memory_space=pltpu.VMEM),
-        scratch_shapes=[
-            pltpu.VMEM((row_tiles, positions, channels), jnp.bfloat16),
-            pltpu.VMEM((positions, channels), jnp.bfloat16),
-            pltpu.VMEM((positions, 1), jnp.float32),
-            pltpu.VMEM((positions, 1), jnp.float32),
-            pltpu.VMEM((positions, channels), jnp.float32),
-            pltpu.SemaphoreType.DMA((2, half + 1, pieces)),
-            pltpu.SemaphoreType.DMA((2, half + 1, pieces)),
-        ],
+        scratch_shapes=ring_scratch(row_tiles, pieces, positions, channels),
         compiler_params=pltpu.CompilerParams(
             collective_id=0, has_side_effects=True, vmem_limit_bytes=40 * 2**20
         ),
     )(normed, residual, *weights)
+
+
+def block_kernel(
+    row_tiles,
+    pieces,
+    latent_ref,
+    cache_ref,
+    gain_ref,
+    kernel_ref,
+    gain2_ref,
+    wq,
+    wk,
+    wv,
+    wo,
+    out_ref,
+    held,
+    queries,
+    highest,
+    total,
+    acc,
+    send_sem,
+    recv_sem,
+    stack,
+    taps,
+    conv,
+    residual,
+    tap_sem,
+    out_sem,
+    row_sem,
+):
+    rows, cols, channels = latent_ref.shape
+    positions = rows * cols
+    me = lax.axis_index("tile")
+    frame = lax.rem(me, 2)
+    tile = lax.div(me, 2)
+    other = me + 1 - 2 * frame
+    ring_left, ring_right = ring_neighbours(tile, row_tiles)
+
+    def wrapped(by):
+        return lax.rem(tile + by + row_tiles, row_tiles) * 2 + frame
+
+    barrier = pltpu.get_barrier_semaphore()
+    for partner in (wrapped(1), wrapped(-1), wrapped(2), wrapped(-2), other):
+        pl.semaphore_signal(barrier, inc=1, device_id={"tile": partner}, device_id_type=MESH)
+
+    def tap_copy(t, i, j):
+        return pltpu.make_async_copy(
+            kernel_ref.at[t, i, j],
+            taps.at[t, i * channels : (i + 1) * channels, j * channels : (j + 1) * channels],
+            tap_sem.at[t, i, j],
+        )
+
+    every = [(i, j) for i in range(3) for j in range(3)]
+    for t in (2, 0, 1):
+        for i, j in every:
+            tap_copy(t, i, j).start()
+
+    first, last = tile == 0, tile == row_tiles - 1
+    owned = lax.rem(tile + 1, row_tiles)
+
+    def send(source, slot, row, number, device):
+        return pltpu.make_async_remote_copy(
+            src_ref=source,
+            dst_ref=stack.at[slot, row],
+            send_sem=out_sem.at[number],
+            recv_sem=row_sem.at[slot, row],
+            device_id={"tile": device},
+            device_id_type=MESH,
+        )
+
+    cache_rows = [send(cache_ref.at[j], 0, 1 + j, j, wrapped(1)) for j in range(rows)]
+    cache_rim = send(cache_ref.at[rows - 1], 0, 0, rows, wrapped(2))
+    rim_down = send(stack.at[2, rows], 2, 0, rows + 1, wrapped(1))
+    rim_up = send(stack.at[2, 1], 2, rows + 1, rows + 2, wrapped(-1))
+    shared = 2 - 2 * frame
+    onward = [send(stack.at[shared, j], 1, j, rows + 3 + j, other) for j in range(rows + 2)]
+
+    pl.semaphore_wait(barrier, 5)
+    for copy in cache_rows:
+        copy.start()
+
+    @pl.when(owned + 1 < row_tiles)
+    def _():
+        cache_rim.start()
+
+    floats = latent_ref[...].astype(jnp.float32)
+    scaled = (
+        floats
+        * lax.rsqrt(jnp.mean(floats * floats, axis=-1, keepdims=True) + 1e-06)
+        * gain_ref[...]
+    )
+    stack[2, 1 : rows + 1] = (scaled / (1.0 + jnp.exp(-scaled))).astype(jnp.bfloat16)
+
+    @pl.when(jnp.logical_not(last))
+    def _():
+        rim_down.start()
+
+    @pl.when(jnp.logical_not(first))
+    def _():
+        rim_up.start()
+
+    @pl.when(frame == 0)
+    def _():
+        for j in range(1, rows + 1):
+            onward[j].start()
+
+    nothing = jnp.zeros((cols, channels), jnp.bfloat16)
+
+    @pl.when(first)
+    def _():
+        stack[0, 0] = nothing
+        stack[2, 0] = nothing
+
+    @pl.when(last)
+    def _():
+        stack[0, rows + 1] = nothing
+        stack[2, rows + 1] = nothing
+
+    @pl.when(jnp.logical_not(last))
+    def _():
+        stack[0, rows + 1] = cache_ref[0]
+
+    def arrived(slot, row):
+        send(stack.at[slot, row], slot, row, 0, other).wait_recv()
+
+    def cached_in():
+        for j in range(1, rows + 1):
+            arrived(0, j)
+            yield j
+
+        @pl.when(jnp.logical_not(first))
+        def _():
+            arrived(0, 0)
+
+        yield 0
+
+    def step(turn, carry):
+        slot = jnp.where(turn == 0, 2, jnp.where(turn == 1, frame, 1 - frame))
+
+        @pl.when(turn == 0)
+        def _():
+            @pl.when(jnp.logical_not(first))
+            def _():
+                arrived(2, 0)
+
+            @pl.when(jnp.logical_not(last))
+            def _():
+                arrived(2, rows + 1)
+
+            @pl.when(frame == 0)
+            def _():
+                onward[0].start()
+                onward[rows + 1].start()
+
+            @pl.when(frame == 1)
+            def _():
+                onward[rows + 1].start()
+
+        @pl.when(jnp.logical_and(turn > 0, slot == 1))
+        def _():
+            for j in range(rows + 2):
+                arrived(1, j)
+
+        @pl.when(jnp.logical_and(turn > 0, jnp.logical_and(slot == 0, frame == 0)))
+        def _():
+            for j in cached_in():
+                pass
+
+        @pl.when(jnp.logical_and(turn > 0, jnp.logical_and(slot == 0, frame == 1)))
+        def _():
+            for j in cached_in():
+                onward[j].start()
+
+        for i, j in every:
+            pltpu.make_async_copy(
+                kernel_ref.at[slot, i, j],
+                taps.at[
+                    slot, i * channels : (i + 1) * channels, j * channels : (j + 1) * channels
+                ],
+                tap_sem.at[slot, i, j],
+            ).wait()
+
+        window = jnp.concatenate(
+            [stack[slot, i : i + rows].reshape(positions, channels) for i in range(3)], axis=-1
+        )
+        product = dot32(window, taps[slot])
+
+        @pl.when(turn == 0)
+        def _():
+            conv[...] = product
+
+        @pl.when(turn > 0)
+        def _():
+            conv[...] += product
+
+        return carry
+
+    lax.fori_loop(0, 3, step, 0)
+
+    column = lax.rem(lax.broadcasted_iota(jnp.int32, (positions, 1), 0), cols)
+    before = pltpu.roll(conv[:, :channels], 1, 0)
+    after = pltpu.roll(conv[:, 2 * channels :], positions - 1, 0)
+    summed = (
+        jnp.where(column == 0, 0.0, before)
+        + conv[:, channels : 2 * channels]
+        + jnp.where(column == cols - 1, 0.0, after)
+    )
+    rounded = (
+        latent_ref[...].reshape(positions, channels).astype(jnp.float32) + summed
+    ).astype(jnp.bfloat16)
+    residual[...] = rounded
+    wide = rounded.astype(jnp.float32)
+    held[0] = (
+        wide * lax.rsqrt(jnp.mean(wide * wide, axis=-1, keepdims=True) + 1e-06) * gain2_ref[...]
+    ).astype(jnp.bfloat16)
+
+    attend_ring(
+        row_tiles,
+        pieces,
+        ring_left * 2 + frame,
+        ring_right * 2 + frame,
+        residual,
+        wq,
+        wk,
+        wv,
+        wo,
+        out_ref,
+        held,
+        queries,
+        highest,
+        total,
+        acc,
+        send_sem,
+        recv_sem,
+    )
+
+    for copy in cache_rows + onward:
+        copy.wait_send()
+
+    @pl.when(owned + 1 < row_tiles)
+    def _():
+        cache_rim.wait_send()
+
+    @pl.when(jnp.logical_not(last))
+    def _():
+        rim_down.wait_send()
+
+    @pl.when(jnp.logical_not(first))
+    def _():
+        rim_up.wait_send()
+
+
+def whole_block(latent, cache, norm_gain, conv_kernel, attend_gain, weights, row_tiles, pieces=2):
+    rows, cols, channels = latent.shape
+    positions = rows * cols
+    held_in_vmem = pl.BlockSpec(memory_space=pltpu.VMEM)
+    return pl.pallas_call(
+        functools.partial(block_kernel, row_tiles, pieces),
+        out_shape=jax.ShapeDtypeStruct((positions, channels), jnp.bfloat16),
+        in_specs=[held_in_vmem] * 3 + [pl.BlockSpec(memory_space=pl.ANY)] + [held_in_vmem] * 5,
+        out_specs=held_in_vmem,
+        scratch_shapes=ring_scratch(row_tiles, pieces, positions, channels)
+        + [
+            pltpu.VMEM((3, rows + 2, cols, channels), jnp.bfloat16),
+            pltpu.VMEM((3, 3 * channels, 3 * channels), jnp.bfloat16),
+            pltpu.VMEM((positions, 3 * channels), jnp.float32),
+            pltpu.VMEM((positions, channels), jnp.bfloat16),
+            pltpu.SemaphoreType.DMA((3, 3, 3)),
+            pltpu.SemaphoreType.DMA((2 * rows + 5,)),
+            pltpu.SemaphoreType.DMA((3, rows + 2)),
+        ],
+        compiler_params=pltpu.CompilerParams(
+            collective_id=0, has_side_effects=True, vmem_limit_bytes=56 * 2**20
+        ),
+    )(
+        latent,
+        cache,
+        norm_gain.reshape(1, channels),
+        conv_kernel,
+        attend_gain.reshape(1, channels),
+        *weights,
+    )
 
 
 def body(
@@ -204,6 +505,17 @@
     tiles = lax.axis_size("tile")
     row_tiles = min(16, tiles // 2)
     frames = tiles // row_tiles
+    if frames == 2 and row_tiles > 4:
+        result = whole_block(
+            video_latent,
+            conv_cache,
+            norm_gain,
+            conv_kernel,
+            attend_gain,
+            (w_query, w_key, w_value, w_output),
+            row_tiles,
+        )
+        return result.reshape(video_latent.shape)
     position = lax.axis_index("tile")
     time_group = position % frames
     activated = jax.nn.silu(rms_scale(video_latent, norm_gain)).astype(jnp.bfloat16)

time: 98.7 us -> 67.2 us (0.68)
  waiting for transfers between devices: 35.5 us -> 0 us
  Pallas kernels: 36.2 us -> 62.8 us
  matrix products: 12.9 us -> 0 us
  other arithmetic: 7.3 us -> 0 us
  starting transfers between devices: 3.11 us -> 0 us
  local copies, waits for them, and re-layouts: 2.83 us -> 4.23 us
    ppermute x4 -> x0, waiting for transfers between devices: 35.5 us -> none  [the longest x2 26.4 us: from_behind(): return lax.ppermute(value, axis, pairs)]
    pallas_call x1, Pallas kernels: 36.2 us -> 62.8 us  [whole_block(): pl.pallas_call(functools.partial(block_kernel, row_tiles, pieces), out_sh...]
    dot_general x27 -> x0, matrix products: 12.9 us -> none  [dot32(): return jnp.dot(a, b, preferred_element_type=jnp.float32)]
    ppermute x4 -> x0, starting transfers between devices: 3.11 us -> none  [the longest x2 2.6 us: passed_along(): return lax.ppermute(block, axis, route)]
    reshape x0 -> x2, local copies, waits for them, and re-layouts: none -> 2.47 us  [the longest x1 1.24 us: whole_block(): norm_gain.reshape(1, channels)]
    another operation x2 -> x0, other arithmetic: 2.37 us -> none  [body(): frame_pair = jnp.stack([activated, conv_cache])]
    concatenate x1 -> x0, other arithmetic: 1.54 us -> none  [body(): stacked = jnp.concatenate([rim_above, stacked, rim_below], axis=1)]
    convert_element_type x2 -> x0, other arithmetic: 1.44 us -> none  [the longest x1 1.28 us: body(): jax.nn.silu(rms_scale(video_latent, norm_gain)).astype(jnp.bfloat16)]
  transfers between devices with their start and end apart: 4 -> 0, of which waited for: 3 -> 0; matrix products, arithmetic and copies ran while one was open for 4% -> 0% of each run, Pallas kernels for 0% -> 0%
where the time goes in v2:
time: 67.2 us; the launch traced here: 67 us
  Pallas kernels  62.8 us (93%)
  local copies, waits for them, and re-layouts  4.23 us (6%)
    pallas_call x1, Pallas kernels, whole_block(): pl.pallas_call(functools.partial(block_kernel, row_tiles, pieces), out_sh...  62.8 us
    unnamed x1, local copies, waits for them, and re-layouts  1.76 us

profile of v2, /device:TPU:0, one launch (start us, length us, event | category | flops | bytes accessed | tf_op | source)
XLA Modules:
  0.0 67.0 jit_solution(13440645043220905539)
XLA Ops:
  0.0 1.2 %reshape.9.gain_ref = f32[1,384]{1,0:T(1,128)} reshape(f32[384]{0:T(512)} %param.11) | data formatting | bytes 3072 | tf_op jit(solution)/shard_map/reshape | solution.py:494
  1.2 1.2 %reshape.10.gain2_ref = f32[1,384]{1,0:T(1,128)} reshape(f32[384]{0:T(512)} %param.13) | data formatting | bytes 3072 | tf_op jit(solution)/shard_map/reshape | solution.py:496
  2.5 62.8 %shard_map.91 = bf16[480,384]{1,0:T(8,128)(2,1)} custom-call(bf16[3,160,384]{2,1,0:T(8,128)(2,1)} %latent_ref.1, bf16[3,160,384]{2,1,0:T(8,128)(2,1)} %cache_ref.1, f32[1,384]{1,0:T(1,128)} %reshape.9.gain_ref, bf16[3,3,3,384,384]{4,3,2,1,0:T(8,128)(2,1)} %kernel_ref.1, f32[1,384]{1,0:T(1,128)} %reshape.10.gain2_ref, bf16[384,384]{1,0:T(8,128)(2,1)} %wq.1, ...), custom_call_target="tpu_custom_call" | custom-call | tf_op jit(solution)/shard_map/pallas_call | solution.py:473
  65.2 1.8 %copy.11 = bf16[3,160,384]{2,1,0:T(8,128)(2,1)} copy(bf16[3,160,384]{2,1,0:T(8,128)(2,1)} %bitcast.1) | data formatting | bytes 737280

commit v3 on v2

--- a/solution.py
+++ b/solution.py
@@ -219,15 +219,15 @@
 def block_kernel(
     row_tiles,
     pieces,
-    latent_ref,
+    latent_hbm,
     cache_ref,
-    gain_ref,
+    gain_hbm,
     kernel_ref,
-    gain2_ref,
-    wq,
-    wk,
-    wv,
-    wo,
+    gain2_hbm,
+    wq_hbm,
+    wk_hbm,
+    wv_hbm,
+    wo_hbm,
     out_ref,
     held,
     queries,
@@ -240,11 +240,19 @@
     taps,
     conv,
     residual,
+    wq,
+    wk,
+    wv,
+    wo,
+    latent_ref,
+    gain_ref,
+    gain2_ref,
     tap_sem,
+    weight_sem,
     out_sem,
     row_sem,
 ):
-    rows, cols, channels = latent_ref.shape
+    rows, cols, channels = latent_hbm.shape
     positions = rows * cols
     me = lax.axis_index("tile")
     frame = lax.rem(me, 2)
@@ -259,6 +267,15 @@
     for partner in (wrapped(1), wrapped(-1), wrapped(2), wrapped(-2), other):
         pl.semaphore_signal(barrier, inc=1, device_id={"tile": partner}, device_id_type=MESH)
 
+    early = [
+        pltpu.make_async_copy(source, target, weight_sem.at[5 + number])
+        for number, (source, target) in enumerate(
+            ((latent_hbm, latent_ref), (gain_hbm, gain_ref), (gain2_hbm, gain2_ref))
+        )
+    ]
+    for load in early:
+        load.start()
+
     def tap_copy(t, i, j):
         return pltpu.make_async_copy(
             kernel_ref.at[t, i, j],
@@ -270,6 +287,14 @@
     for t in (2, 0, 1):
         for i, j in every:
             tap_copy(t, i, j).start()
+    loads = [
+        pltpu.make_async_copy(source, target, weight_sem.at[number])
+        for number, (source, target) in enumerate(
+            ((wq_hbm, wq), (wk_hbm, wk), (wv_hbm, wv), (wo_hbm, wo))
+        )
+    ]
+    for load in loads:
+        load.start()
 
     first, last = tile == 0, tile == row_tiles - 1
     owned = lax.rem(tile + 1, row_tiles)
@@ -291,19 +316,21 @@
     shared = 2 - 2 * frame
     onward = [send(stack.at[shared, j], 1, j, rows + 3 + j, other) for j in range(rows + 2)]
 
+    own_rim = pltpu.make_async_copy(cache_ref.at[0], stack.at[0, rows + 1], weight_sem.at[4])
     pl.semaphore_wait(barrier, 5)
-    for copy in cache_rows:
-        copy.start()
+    cache_rows[0].start()
 
     @pl.when(owned + 1 < row_tiles)
     def _():
         cache_rim.start()
 
+    for load in early:
+        load.wait()
     floats = latent_ref[...].astype(jnp.float32)
     scaled = (
         floats
         * lax.rsqrt(jnp.mean(floats * floats, axis=-1, keepdims=True) + 1e-06)
-        * gain_ref[...]
+        * gain_ref[...].reshape(1, 1, channels)
     )
     stack[2, 1 : rows + 1] = (scaled / (1.0 + jnp.exp(-scaled))).astype(jnp.bfloat16)
 
@@ -320,6 +347,9 @@
         for j in range(1, rows + 1):
             onward[j].start()
 
+    for copy in cache_rows[1:]:
+        copy.start()
+
     nothing = jnp.zeros((cols, channels), jnp.bfloat16)
 
     @pl.when(first)
@@ -334,7 +364,8 @@
 
     @pl.when(jnp.logical_not(last))
     def _():
-        stack[0, rows + 1] = cache_ref[0]
+        own_rim.start()
+        own_rim.wait()
 
     def arrived(slot, row):
         send(stack.at[slot, row], slot, row, 0, other).wait_recv()
@@ -427,9 +458,13 @@
     residual[...] = rounded
     wide = rounded.astype(jnp.float32)
     held[0] = (
-        wide * lax.rsqrt(jnp.mean(wide * wide, axis=-1, keepdims=True) + 1e-06) * gain2_ref[...]
+        wide
+        * lax.rsqrt(jnp.mean(wide * wide, axis=-1, keepdims=True) + 1e-06)
+        * gain2_ref[...].reshape(1, channels)
     ).astype(jnp.bfloat16)
 
+    for load in loads:
+        load.wait()
     attend_ring(
         row_tiles,
         pieces,
@@ -473,7 +508,7 @@
     return pl.pallas_call(
         functools.partial(block_kernel, row_tiles, pieces),
         out_shape=jax.ShapeDtypeStruct((positions, channels), jnp.bfloat16),
-        in_specs=[held_in_vmem] * 3 + [pl.BlockSpec(memory_space=pl.ANY)] + [held_in_vmem] * 5,
+        in_specs=[pl.BlockSpec(memory_space=pltpu.HBM)] * 9,
         out_specs=held_in_vmem,
         scratch_shapes=ring_scratch(row_tiles, pieces, positions, channels)
         + [
@@ -481,19 +516,26 @@
             pltpu.VMEM((3, 3 * channels, 3 * channels), jnp.bfloat16),
             pltpu.VMEM((positions, 3 * channels), jnp.float32),
             pltpu.VMEM((positions, channels), jnp.bfloat16),
+        ]
+        + [pltpu.VMEM((channels, channels), jnp.bfloat16)] * 4
+        + [
+            pltpu.VMEM((rows, cols, channels), jnp.bfloat16),
+            pltpu.VMEM((channels,), jnp.float32),
+            pltpu.VMEM((channels,), jnp.float32),
             pltpu.SemaphoreType.DMA((3, 3, 3)),
+            pltpu.SemaphoreType.DMA((8,)),
             pltpu.SemaphoreType.DMA((2 * rows + 5,)),
             pltpu.SemaphoreType.DMA((3, rows + 2)),
         ],
         compiler_params=pltpu.CompilerParams(
-            collective_id=0, has_side_effects=True, vmem_limit_bytes=56 * 2**20
+            collective_id=0, has_side_effects=True, vmem_limit_bytes=36 * 2**20
         ),
     )(
         latent,
         cache,
-        norm_gain.reshape(1, channels),
+        norm_gain,
         conv_kernel,
-        attend_gain.reshape(1, channels),
+        attend_gain,
         *weights,
     )
 

time: 67.2 us -> 68.6 us (1.021)
  local copies, waits for them, and re-layouts: 4.23 us -> 11.2 us
  Pallas kernels: 62.8 us -> 57 us
    unnamed x1 -> x19, local copies, waits for them, and re-layouts: 1.76 us -> 11.2 us
    pallas_call x1, Pallas kernels: 62.8 us -> 57 us  [whole_block(): pl.pallas_call(functools.partial(block_kernel, row_tiles, pieces), out_sh...]
    reshape x2 -> x0, local copies, waits for them, and re-layouts: 2.47 us -> none  [the longest x1 1.24 us: whole_block(): norm_gain.reshape(1, channels)]
where the time goes in v3:
time: 68.6 us; the launch traced here: 68.2 us
  Pallas kernels  57 us (83%)
  local copies, waits for them, and re-layouts  11.2 us (16%)
    pallas_call x1, Pallas kernels, whole_block(): pl.pallas_call(functools.partial(block_kernel, row_tiles, pieces), out_sh...  57 us
    unnamed x19, local copies, waits for them, and re-layouts  11.2 us

profile of v3, /device:TPU:0, one launch (start us, length us, event | category | flops | bytes accessed | tf_op | source)
XLA Modules:
  0.0 68.2 jit_solution(17375455643233598906)
XLA Ops:
  0.0 0.0 copy-start
  0.0 3.3 %copy-done = bf16[3,3,3,384,384]{4,3,2,1,0:T(8,128)(2,1)S(1)} copy-done((bf16[3,3,3,384,384]{4,3,2,1,0:T(8,128)(2,1)S(1)}, bf16[3,3,3,384,384]{4,3,2,1,0:T(8,128)(2,1)}, u32[]{:S(2)}) %copy-start) | copy-done | bytes 7962648
  3.3 0.0 copy-start.1
  3.3 1.0 %copy-done.1 = bf16[3,160,384]{2,1,0:T(8,128)(2,1)S(1)} copy-done((bf16[3,160,384]{2,1,0:T(8,128)(2,1)S(1)}, bf16[3,160,384]{2,1,0:T(8,128)(2,1)}, u32[]{:S(2)}) %copy-start.1) | copy-done | bytes 368664
  4.2 0.0 copy-start.2
  4.3 1.0 %copy-done.2 = bf16[3,160,384]{2,1,0:T(8,128)(2,1)S(1)} copy-done((bf16[3,160,384]{2,1,0:T(8,128)(2,1)S(1)}, bf16[3,160,384]{2,1,0:T(8,128)(2,1)}, u32[]{:S(2)}) %copy-start.2) | copy-done | bytes 368664
  5.2 0.0 copy-start.3
  5.2 1.0 %copy-done.3 = bf16[384,384]{1,0:T(8,128)(2,1)S(1)} copy-done((bf16[384,384]{1,0:T(8,128)(2,1)S(1)}, bf16[384,384]{1,0:T(8,128)(2,1)}, u32[]{:S(2)}) %copy-start.3) | copy-done | bytes 294936
  6.2 0.0 copy-start.4
  6.2 1.0 %copy-done.4 = bf16[384,384]{1,0:T(8,128)(2,1)S(1)} copy-done((bf16[384,384]{1,0:T(8,128)(2,1)S(1)}, bf16[384,384]{1,0:T(8,128)(2,1)}, u32[]{:S(2)}) %copy-start.4) | copy-done | bytes 294936
  7.2 0.0 copy-start.5
  7.2 1.0 %copy-done.5 = bf16[384,384]{1,0:T(8,128)(2,1)S(1)} copy-done((bf16[384,384]{1,0:T(8,128)(2,1)S(1)}, bf16[384,384]{1,0:T(8,128)(2,1)}, u32[]{:S(2)}) %copy-start.5) | copy-done | bytes 294936
  8.1 0.0 copy-start.6
  8.1 1.0 %copy-done.6 = bf16[384,384]{1,0:T(8,128)(2,1)S(1)} copy-done((bf16[384,384]{1,0:T(8,128)(2,1)S(1)}, bf16[384,384]{1,0:T(8,128)(2,1)}, u32[]{:S(2)}) %copy-start.6) | copy-done | bytes 294936
  9.1 0.0 copy-start.7
  9.1 0.7 copy-done.7
  9.8 0.0 copy-start.8
  9.8 0.7 copy-done.8
  10.4 57.0 %shard_map.91 = bf16[480,384]{1,0:T(8,128)(2,1)S(1)} custom-call(bf16[3,160,384]{2,1,0:T(8,128)(2,1)S(1)} %copy-done.1, bf16[3,160,384]{2,1,0:T(8,128)(2,1)S(1)} %copy-done.2, f32[384]{0:T(512)S(1)} %copy-done.7, bf16[3,3,3,384,384]{4,3,2,1,0:T(8,128)(2,1)S(1)} %copy-done, f32[384]{0:T(512)S(1)} %copy-done.8, bf16[384,384]{1,0:T(8,128)(2,1)S(1)} %copy-done.3, ...), custom_call_target="tpu_custom_call" | custom-call | tf_op jit(solution)/shard_map/pallas_call | solution.py:508
  67.4 0.7 %copy.11 = bf16[3,160,384]{2,1,0:T(8,128)(2,1)} copy(bf16[3,160,384]{2,1,0:T(8,128)(2,1)S(1)} %bitcast.1) | data formatting | bytes 737280
Async XLA Ops:
  0.0 3.3 %copy-start = (bf16[3,3,3,384,384]{4,3,2,1,0:T(8,128)(2,1)S(1)}, bf16[3,3,3,384,384]{4,3,2,1,0:T(8,128)(2,1)}, u32[]{:S(2)}) copy-start(bf16[3,3,3,384,384]{4,3,2,1,0:T(8,128)(2,1)} %kernel_ref.1) | copy-start | bytes 23887876
  3.3 1.0 %copy-start.1 = (bf16[3,160,384]{2,1,0:T(8,128)(2,1)S(1)}, bf16[3,160,384]{2,1,0:T(8,128)(2,1)}, u32[]{:S(2)}) copy-start(bf16[3,160,384]{2,1,0:T(8,128)(2,1)} %latent_hbm.1) | copy-start | bytes 1105924
  4.2 1.0 %copy-start.2 = (bf16[3,160,384]{2,1,0:T(8,128)(2,1)S(1)}, bf16[3,160,384]{2,1,0:T(8,128)(2,1)}, u32[]{:S(2)}) copy-start(bf16[3,160,384]{2,1,0:T(8,128)(2,1)} %cache_ref.1) | copy-start | bytes 1105924
  5.2 1.0 %copy-start.3 = (bf16[384,384]{1,0:T(8,128)(2,1)S(1)}, bf16[384,384]{1,0:T(8,128)(2,1)}, u32[]{:S(2)}) copy-start(bf16[384,384]{1,0:T(8,128)(2,1)} %wq_hbm.1) | copy-start | bytes 884740
  6.2 1.0 %copy-start.4 = (bf16[384,384]{1,0:T(8,128)(2,1)S(1)}, bf16[384,384]{1,0:T(8,128)(2,1)}, u32[]{:S(2)}) copy-start(bf16[384,384]{1,0:T(8,128)(2,1)} %wk_hbm.1) | copy-start | bytes 884740
  7.2 1.0 %copy-start.5 = (bf16[384,384]{1,0:T(8,128)(2,1)S(1)}, bf16[384,384]{1,0:T(8,128)(2,1)}, u32[]{:S(2)}) copy-start(bf16[384,384]{1,0:T(8,128)(2,1)} %wv_hbm.1) | copy-start | bytes 884740
  8.1 1.0 %copy-start.6 = (bf16[384,384]{1,0:T(8,128)(2,1)S(1)}, bf16[384,384]{1,0:T(8,128)(2,1)}, u32[]{:S(2)}) copy-start(bf16[384,384]{1,0:T(8,128)(2,1)} %wo_hbm.1) | copy-start | bytes 884740
  9.1 0.7 copy-start.7
  9.8 0.7 copy-start.8

commit v4 on v3

--- a/solution.py
+++ b/solution.py
@@ -528,7 +528,7 @@
             pltpu.SemaphoreType.DMA((3, rows + 2)),
         ],
         compiler_params=pltpu.CompilerParams(
-            collective_id=0, has_side_effects=True, vmem_limit_bytes=36 * 2**20
+            collective_id=0, has_side_effects=True, vmem_limit_bytes=58 * 2**20
         ),
     )(
         latent,

time: 68.6 us -> 61.7 us (0.90)
  local copies, waits for them, and re-layouts: 11.2 us -> 1.76 us
  Pallas kernels: 57 us -> 59.8 us
    unnamed x19 -> x1, local copies, waits for them, and re-layouts: 11.2 us -> 1.76 us
    pallas_call x1, Pallas kernels: 57 us -> 59.8 us  [whole_block(): pl.pallas_call(functools.partial(block_kernel, row_tiles, pieces), out_sh...]
where the time goes in v4:
time: 61.7 us; the launch traced here: 61.6 us
  Pallas kernels  59.8 us (97%)
  local copies, waits for them, and re-layouts  1.76 us (3%)
    pallas_call x1, Pallas kernels, whole_block(): pl.pallas_call(functools.partial(block_kernel, row_tiles, pieces), out_sh...  59.8 us
    unnamed x1, local copies, waits for them, and re-layouts  1.76 us

profile of v4, /device:TPU:0, one launch (start us, length us, event | category | flops | bytes accessed | tf_op | source)
XLA Modules:
  0.0 61.6 jit_solution(8763912742072921450)
XLA Ops:
  0.0 59.8 %shard_map.91 = bf16[480,384]{1,0:T(8,128)(2,1)} custom-call(bf16[3,160,384]{2,1,0:T(8,128)(2,1)} %latent_hbm.1, bf16[3,160,384]{2,1,0:T(8,128)(2,1)} %cache_ref.1, f32[384]{0:T(512)} %gain_hbm.1, bf16[3,3,3,384,384]{4,3,2,1,0:T(8,128)(2,1)} %kernel_ref.1, f32[384]{0:T(512)} %gain2_hbm.1, bf16[384,384]{1,0:T(8,128)(2,1)} %wq_hbm.1, bf16[384,384]{1,0:T(8,128)(2,1)} %wk_hbm.1, ...), custom_call_target="tpu_custom_call" | custom-call | tf_op jit(solution)/shard_map/pallas_call | solution.py:508
  59.8 1.8 %copy.11 = bf16[3,160,384]{2,1,0:T(8,128)(2,1)} copy(bf16[3,160,384]{2,1,0:T(8,128)(2,1)} %bitcast.1) | data formatting | bytes 737280

commit v5 on v4

--- a/solution.py
+++ b/solution.py
@@ -284,9 +284,9 @@
         )
 
     every = [(i, j) for i in range(3) for j in range(3)]
-    for t in (2, 0, 1):
+    for turn in range(3):
         for i, j in every:
-            tap_copy(t, i, j).start()
+            tap_copy(jnp.where(frame == 0, 2 - turn, turn), i, j).start()
     loads = [
         pltpu.make_async_copy(source, target, weight_sem.at[number])
         for number, (source, target) in enumerate(
@@ -318,7 +318,11 @@
 
     own_rim = pltpu.make_async_copy(cache_ref.at[0], stack.at[0, rows + 1], weight_sem.at[4])
     pl.semaphore_wait(barrier, 5)
-    cache_rows[0].start()
+
+    @pl.when(frame == 1)
+    def _():
+        for copy in cache_rows:
+            copy.start()
 
     @pl.when(owned + 1 < row_tiles)
     def _():
@@ -347,8 +351,10 @@
         for j in range(1, rows + 1):
             onward[j].start()
 
-    for copy in cache_rows[1:]:
-        copy.start()
+    @pl.when(frame == 0)
+    def _():
+        for copy in cache_rows:
+            copy.start()
 
     nothing = jnp.zeros((cols, channels), jnp.bfloat16)
 
@@ -382,9 +388,9 @@
         yield 0
 
     def step(turn, carry):
-        slot = jnp.where(turn == 0, 2, jnp.where(turn == 1, frame, 1 - frame))
-
-        @pl.when(turn == 0)
+        slot = jnp.where(frame == 0, 2 - turn, turn)
+
+        @pl.when(slot == 2)
         def _():
             @pl.when(jnp.logical_not(first))
             def _():
@@ -399,22 +405,19 @@
                 onward[0].start()
                 onward[rows + 1].start()
 
-            @pl.when(frame == 1)
-            def _():
-                onward[rows + 1].start()
-
-        @pl.when(jnp.logical_and(turn > 0, slot == 1))
+        @pl.when(slot == 1)
         def _():
             for j in range(rows + 2):
                 arrived(1, j)
 
-        @pl.when(jnp.logical_and(turn > 0, jnp.logical_and(slot == 0, frame == 0)))
+        @pl.when(jnp.logical_and(slot == 0, frame == 0))
         def _():
             for j in cached_in():
                 pass
 
-        @pl.when(jnp.logical_and(turn > 0, jnp.logical_and(slot == 0, frame == 1)))
+        @pl.when(jnp.logical_and(slot == 0, frame == 1))
         def _():
+            onward[rows + 1].start()
             for j in cached_in():
                 onward[j].start()
 

time: 61.7 us -> 61.4 us (level)
  no operation moved by 1% of the time
where the time goes in v5:
time: 61.4 us; the launch traced here: 61.3 us
  Pallas kernels  59.5 us (97%)
  local copies, waits for them, and re-layouts  1.76 us (3%)
    pallas_call x1, Pallas kernels, whole_block(): pl.pallas_call(functools.partial(block_kernel, row_tiles, pieces), out_sh...  59.5 us
    unnamed x1, local copies, waits for them, and re-layouts  1.76 us

profile of v5, /device:TPU:0, one launch (start us, length us, event | category | flops | bytes accessed | tf_op | source)
XLA Modules:
  0.0 61.3 jit_solution(1190780963700243344)
XLA Ops:
  0.0 59.5 %shard_map.91 = bf16[480,384]{1,0:T(8,128)(2,1)} custom-call(bf16[3,160,384]{2,1,0:T(8,128)(2,1)} %latent_hbm.1, bf16[3,160,384]{2,1,0:T(8,128)(2,1)} %cache_ref.1, f32[384]{0:T(512)} %gain_hbm.1, bf16[3,3,3,384,384]{4,3,2,1,0:T(8,128)(2,1)} %kernel_ref.1, f32[384]{0:T(512)} %gain2_hbm.1, bf16[384,384]{1,0:T(8,128)(2,1)} %wq_hbm.1, bf16[384,384]{1,0:T(8,128)(2,1)} %wk_hbm.1, ...), custom_call_target="tpu_custom_call" | custom-call | tf_op jit(solution)/shard_map/pallas_call | solution.py:511
  59.5 1.8 %copy.11 = bf16[3,160,384]{2,1,0:T(8,128)(2,1)} copy(bf16[3,160,384]{2,1,0:T(8,128)(2,1)} %bitcast.1) | data formatting | bytes 737280
